TPU v7x, 32 devices: a whole 2x2x4 slice. The times are simulated.
32 devices in a mesh: gx: 8 (over z, core), gy: 4 (over y, x).
Axes of the slice: x: 2, y: 2, z: 4, core: 2. Of those that a mesh axis runs over, the one named last changes fastest.
Arguments:
- right_side: float32 [128, 128, 128], P('gx', 'gy'), may hold values from -1 to 2
- screening: float32 [128, 128, 128], P('gx', 'gy'), may hold values from 0.5 to 5
- active_blocks: int32 [8, 4, 12], P('gx', 'gy'), may hold values from -1 to 15, as said below
- visible_bricks: int32 [8, 4, 8], P('gx', 'gy'), may hold values from -1 to 15, as said below
Outputs:
- indicator: float32 [128, 128, 128], P('gx', 'gy')
- crossing: float32 [64, 4, 3, 4096], P('gx', 'gy')
Inputs may be any that keep to these rules, and one draw needn't show every extreme that they name: `active_blocks`: each device's row lists distinct block numbers of that device's 16 blocks first, then -1 in the unused slots; at least one entry is a block number; some device fills all 12 slots and some leaves slots unused. `visible_bricks`: each device's row lists distinct block numbers of that device's 16 blocks first, then -1 in the unused slots; at least one entry is a block number; some device fills all 8 slots.
All inputs are finite; a program needn't handle non-finite values.
Results may differ from a plain program's by a relative error of at most 0.0003.
Values sent between devices are 32-bit elements; how exact they have to be, the bound alone decides.
No kernel may reach another device: no remote copies, remote signals or barrier semaphores. Data moves between devices by JAX's collectives and lax.ppermute only.
A program may use at most 64 MiB of HBM per device.

v0:
```python
import functools

import jax
import jax.numpy as jnp
from jax import lax
from jax.experimental import pallas as pl
from jax.experimental.pallas import tpu as pltpu
from jax.sharding import PartitionSpec as P

BLK = 16
WIDE = 5
NEAR = 3
HEM = 4
EDGE = 8
SHARP = 4.0
SCALE = 1.0 / 86400.0
SHIFT = 2.25
LOW, HIGH = 0.5, 7.0
SUMS = 16
EXTRA, INNER, SIDE = 96, 0, 0
HELD = 11
F32 = jnp.float32


def mass(mid, one, two):
    return 66.0 * mid + (26.0 * one + two)


def stiff(mid, one, two):
    return 6.0 * mid - (2.0 * one + two)


def block_mask(active, slots, rows, columns):
    y = lax.broadcasted_iota(jnp.int32, (rows, columns), 0)
    z = lax.broadcasted_iota(jnp.int32, (rows, columns), 1)
    number = (y // BLK) * (columns // BLK) + z // BLK
    mask = jnp.zeros((rows, columns), F32)
    for slot in range(slots):
        mask = jnp.where(number == active[slot], 1.0, mask)
    return mask


def on_odd():
    return lax.rem(lax.axis_index("gx"), 2)


def odd_on(axis):
    return lax.rem(lax.axis_index(axis), 2)


def pack_kernel(active_hbm, right_hbm, screen_hbm, far, near, mask_out, active, right, screen, sems):
    nx, ny, nz = right_hbm.shape
    copies = [pltpu.make_async_copy(active_hbm, active, sems.at[0])]
    for k, (source, target) in enumerate(((right_hbm, right), (screen_hbm, screen))):
        for high in range(2):
            rows = pl.ds(high * (ny - EDGE), EDGE)
            copies.append(pltpu.make_async_copy(source.at[:, rows], target.at[high], sems.at[1 + 2 * k + high]))
    for copy in copies:
        copy.start()
    copies[0].wait()
    mask = block_mask(active, active.shape[0], ny, nz)
    mask_out[...] = mask
    row = lax.broadcasted_iota(jnp.int32, (EDGE, nz), 0)
    for copy in copies[1:]:
        copy.wait()

    def write(high_out, low_out):
        for x in range(nx):
            rows = pl.ds(x * EDGE, EDGE)
            low_out[rows] = jnp.where(row < WIDE, right[0, x], pltpu.roll(screen[0, x], WIDE, 0)) * mask[:EDGE]
            beside = pltpu.roll(screen[1, x] * mask[ny - EDGE :], NEAR, 0)
            high_out[rows] = jnp.where(row >= NEAR, right[1, x] * mask[ny - EDGE :], beside)

    odd = odd_on("gy")
    pl.when(odd == 1)(functools.partial(write, far, near))
    pl.when(odd == 0)(functools.partial(write, near, far))


def place_kernel(mask_in, right, screen, field, weight, cross, chip):
    nx, ny, nz = right.shape
    mask = mask_in[...]
    own = pl.ds(EDGE, ny)
    for x in range(nx):
        field[WIDE + x, own] = right[x] * mask
        weight[x, own] = screen[x] * mask
    odd = odd_on("gx")
    for target, high in ((cross, odd), (chip, 1 - odd)):
        for x in range(WIDE):
            target[x * ny : (x + 1) * ny] = field[WIDE + high * (nx - WIDE) + x, own]
        for x in range(NEAR):
            row = (WIDE + x) * ny
            target[row : row + ny] = weight[high * (nx - NEAR) + x, own]


def widen_kernel(far, near, chip_in, chip, corner):
    nx = far.shape[0] // EDGE
    base = chip.shape[0] - corner.shape[0]
    odd = odd_on("gx")

    def fill(low, high):
        for target, start, side in ((corner, 0, odd), (chip, base, 1 - odd)):
            for x in range(WIDE):
                tile = pl.ds((side * (nx - WIDE) + x) * EDGE, EDGE)
                row = start + 2 * x * EDGE
                target[row : row + EDGE] = low[tile]
                target[row + EDGE : row + 2 * EDGE] = high[tile]

    by_y(fill, far, near)


def by_y(action, far, near):
    odd = odd_on("gy")
    pl.when(odd == 1)(functools.partial(action, near, far))
    pl.when(odd == 0)(functools.partial(action, far, near))


def near_z(value):
    lane = lax.broadcasted_iota(jnp.int32, value.shape, 1)
    last = value.shape[1]

    def shifted(step):
        before = jnp.where(lane >= step, pltpu.roll(value, step, 1), 0.0)
        after = jnp.where(lane < last - step, pltpu.roll(value, last - step, 1), 0.0)
        return before + after

    return shifted(1), shifted(2)


def set_beside(field, x, keep, shifted, weight_x, tile, high):
    start = field.shape[1] - EDGE if high else 0
    field[x, start : start + EDGE] = tile
    if weight_x is not None:
        set_weight(keep, shifted, weight_x, pl.ds(start, EDGE), pltpu.roll(tile, NEAR if high else WIDE, 0))


def set_weight(keep, shifted, at, rows, weight):
    on = weight > 0.0
    keep[at, rows] = jnp.where(on, SCALE, 0.0)
    shifted[at, rows] = jnp.where(on, weight - SHIFT, 0.0)


def near_y(source, x, row, top, end):
    def part(step):
        return source[x, pl.ds(row + step, 8)]

    below, above = part(-2), part(2)
    place = lax.broadcasted_iota(jnp.int32, below.shape, 0)
    if top:
        below = jnp.where(place == 0, 0.0, jnp.where(place == 1, 2.0 * below, below))
    if end:
        above = jnp.where(place == 7, 0.0, jnp.where(place == 6, 2.0 * above, above))
    return part(0), part(-1) + part(1), below + above


def along_yz(source, x, row, top=False, end=False):
    here, one, two = near_y(source, x, row, top, end)
    heavy, stretched = mass(here, one, two), stiff(here, one, two)
    heavy_near, stretched_near = near_z(heavy), near_z(stretched)
    return mass(heavy, *heavy_near), stiff(heavy, *heavy_near) + mass(stretched, *stretched_near)


def across(window):
    p, q = zip(*window)
    return mass(q[2], q[1] + q[3], q[0] + q[4]) + stiff(p[2], p[1] + p[3], p[0] + p[4])


def power(target, source, row, keep, shifted, skip, x, group, window):
    rows, at = pl.ds(EDGE + 8 * group, 8), pl.ds(EDGE - HEM + 8 * group, 8)
    center = source[x + 2, pl.ds(row + 8 * group, 8)]
    target[x, rows] = keep[x + skip, at] * across(window) + shifted[x + skip, at] * center


def advance(target, source, row, keep, shifted, skip, yp, yq, count, first):
    for group in range(target.shape[1] // 8 - 2):
        rows = pl.ds(8 * group, 8)
        window = []
        for x in range(first, first + count):
            p, q = along_yz(source, x, row + 8 * group)
            yp[x, rows] = p
            yq[x, rows] = q
            window = window[-4:] + [(p, q)]
            if len(window) == 5:
                power(target, source, row, keep, shifted, skip, x - 4, group, window)


def advance_side(target, source, row, keep, shifted, skip, yp, yq, high):
    groups = target.shape[1] // 8 - 2
    base = high * (target.shape[0] - WIDE)
    start = high * (source.shape[0] - WIDE)
    for group in range(groups):
        rows = pl.ds(8 * group, 8)
        for k in range(WIDE):
            p, q = along_yz(source, start + k, row + 8 * group)
            yp[start + k, rows] = p
            yq[start + k, rows] = q
    for group in range(groups):
        rows = pl.ds(8 * group, 8)
        window = [(yp[base + k, rows], yq[base + k, rows]) for k in range(WIDE + 4)]
        for k in range(WIDE):
            power(target, source, row, keep, shifted, skip, base + k, group, window[k : k + 5])


def last_rows(source, yp, yq, count, first):
    groups = yp.shape[1] // 8
    for group in range(groups):
        rows = pl.ds(8 * group, 8)
        for k in range(count):
            p, q = along_yz(source, first + k, EDGE + HEM + 8 * group, group == 0, group == groups - 1)
            yp[first + 1 + k, rows] = p
            yq[first + 1 + k, rows] = q


def fold(value):
    return jnp.sum(value.reshape(-1, 8, value.shape[1]), axis=0)


def add_sums(totals, arrays, count, first_x):
    field, keep, shifted, first, second, yp, yq = arrays
    totals = list(totals)
    for group in range(yp.shape[1] // 8):
        rows = pl.ds(8 * group, 8)
        mid, own = pl.ds(EDGE + 8 * group, 8), pl.ds(EDGE + HEM + 8 * group, 8)
        window = [(yp[first_x + k, rows], yq[first_x + k, rows]) for k in range(count + 4)]
        for k in range(count):
            x = first_x + k
            v0 = field[x + WIDE, mid]
            v1 = first[x + NEAR, own]
            v2 = second[x + 1, own]
            form = v2 * (SCALE * across(window[k : k + 5]) + shifted[x + NEAR, mid] * v2)
            on = jnp.where(keep[x + NEAR, mid] > 0.0, 1.0, 0.0)
            new = (v0 * v0, v0 * v1, v1 * v1, v1 * v2, v2 * v2, form, v0, v1, v2, on)
            totals = [total + value for total, value in zip(totals, new)]
    return totals


def inner_kernel(
    far, near, field_in, weight, field, keep, shifted, first, second, yp1, yq1, yp2, yq2, yp3, yq3, sums
):
    nx, wide, nz = weight.shape
    ny = wide - 2 * EDGE

    def fill(low, high):
        for x in range(nx):
            set_beside(field, WIDE + x, keep, shifted, NEAR + x, low[EDGE * x : EDGE * (x + 1)], False)
            set_beside(field, WIDE + x, keep, shifted, NEAR + x, high[EDGE * x : EDGE * (x + 1)], True)

    by_y(fill, far, near)
    own = pl.ds(EDGE, ny)
    for x in range(nx):
        set_weight(keep, shifted, NEAR + x, own, weight[x, own])
    advance(first, field, EDGE - HEM, keep, shifted, 0, yp1, yq1, nx, WIDE)
    advance(second, first, EDGE, keep, shifted, 2, yp2, yq2, nx - 4, WIDE)
    last_rows(second, yp3, yq3, nx - 8, WIDE)
    arrays = (field, keep, shifted, first, second, yp3, yq3)
    totals = add_sums((jnp.zeros((8, nz), F32),) * 10, arrays, nx - 12, WIDE + 1)
    for place, total in enumerate(totals):
        sums[place] = total


def side_kernel(last, message, corner, *refs):
    sums_in = refs[HELD]
    field, keep, shifted, first, second, yp1, yq1, yp2, yq2, yp3, yq3, sums = refs[HELD + 1 :]
    planes, wide, nz = field.shape
    nx, ny = planes - 2 * WIDE, wide - 2 * EDGE
    odd = odd_on("gx")
    high = odd if last else 1 - odd
    own = pl.ds(EDGE, ny)
    base = corner.shape[0] - 2 * WIDE * EDGE
    for x in range(WIDE):
        plane = high * (nx + WIDE) + x
        field[plane, own] = message[x * ny : (x + 1) * ny]
        for up in range(2):
            row = base + (2 * x + up) * EDGE
            set_beside(field, plane, keep, shifted, None, corner[row : row + EDGE], up == 1)
    for x in range(NEAR):
        plane = high * (nx + NEAR) + x
        row = (WIDE + x) * ny
        set_weight(keep, shifted, plane, own, message[row : row + ny])
        place = base + (x + (1 - high) * (WIDE - NEAR)) * 2 * EDGE
        for up in range(2):
            tile = corner[pl.ds(place + up * EDGE, EDGE)]
            rows = pl.ds(up * (wide - EDGE), EDGE)
            set_weight(keep, shifted, plane, rows, pltpu.roll(tile, NEAR if up else WIDE, 0))
    advance_side(first, field, EDGE - HEM, keep, shifted, 0, yp1, yq1, high)
    advance_side(second, first, EDGE, keep, shifted, 2, yp2, yq2, high)
    last_rows(second, yp3, yq3, WIDE, high * (nx + 2 - WIDE))
    none = jnp.zeros((ny, nz), F32)
    yp3[high * (nx + 3)] = none
    yq3[high * (nx + 3)] = none
    totals = tuple(sums_in[place] for place in range(10))
    arrays = (field, keep, shifted, first, second, yp3, yq3)
    totals = list(add_sums(totals, arrays, WIDE + 1, high * (nx - WIDE - 1)))
    own = pl.ds(EDGE + HEM, ny)
    beside, edge, next_edge = 1 + high * (nx + 1), 2 + high * (nx - 1), 3 + high * (nx - 3)
    give = 13.0 * yq3[edge] - yp3[edge] + (yq3[next_edge] - yp3[next_edge])
    take = 13.0 * yq3[beside] - yp3[beside]
    totals[5] += SCALE * fold(second[beside - 1, own] * give - second[edge - 1, own] * take)
    if not last:
        for place, total in enumerate(totals):
            sums[place] = total
        return
    row = lax.broadcasted_iota(jnp.int32, (SUMS, nz), 0)
    lane = lax.broadcasted_iota(jnp.int32, (SUMS, nz), 1)
    lines = jnp.zeros((SUMS, nz), F32)
    for place, total in enumerate(totals):
        lines = jnp.where(row == place, jnp.sum(total, axis=0, keepdims=True), lines)
    pieces, rest = [], lines
    for _ in range(3):
        pieces.append(rest.astype(jnp.bfloat16))
        rest = rest - pieces[-1].astype(F32)
    ones = jnp.ones((nz, nz), jnp.bfloat16)
    whole_sums = jnp.dot(jnp.concatenate(pieces, axis=0), ones, preferred_element_type=F32)
    top, rest = two_sum(whole_sums[:SUMS], whole_sums[SUMS : 2 * SUMS])
    pair = two_sum(top, rest + whole_sums[2 * SUMS :])
    spot = jnp.where(lane == row, pair[0], jnp.where(lane == row + SUMS, pair[1], 0.0))
    sums[...] = jnp.sum(spot, axis=0, keepdims=True)


def two_sum(a, b):
    total = a + b
    part = total - a
    return total, (a - (total - part)) + (b - part)


def pair_add(a, b):
    total, rest = two_sum(a[0], b[0])
    return total, rest + (a[1] + b[1])


def halves(a):
    wide = 4097.0 * a
    top = wide - (wide - a)
    return top, a - top


def pair_mul(a, b):
    product = a[0] * b[0]
    a_top, a_rest = halves(a[0])
    b_top, b_rest = halves(b[0])
    rest = ((a_top * b_top - product) + a_top * b_rest + a_rest * b_top) + a_rest * b_rest
    rest = rest + (a[0] * b[1] + a[1] * b[0])
    total = product + rest
    return total, rest - (total - product)


def pair_sub(a, b):
    total, rest = two_sum(a[0], -b[0])
    rest = rest + (a[1] - b[1])
    out = total + rest
    return out, rest - (out - total)


def ratio(over, under, low, high):
    good = under > 0.0
    value = jnp.where(good, over / jnp.where(good, under, 1.0), 0.5 * (low + high))
    return jnp.minimum(jnp.maximum(value, low), high)


def coefficients(total):
    scale = 1.0 / total[0][0]
    zero = jnp.zeros_like(scale)
    g = [pair_mul(item, (scale, zero)) for item in total[:6]]
    shift = (jnp.full_like(scale, SHIFT), zero)
    h = [pair_add(g[k + 1], pair_mul(g[k], shift)) for k in range(5)]

    def minor(a, b, c, d):
        return pair_sub(pair_mul(a, b), pair_mul(c, d))

    s11 = minor(h[2], h[0], h[1], h[1])
    s12 = minor(h[3], h[0], h[1], h[2])
    s22 = minor(h[4], h[0], h[2], h[2])
    y1 = minor(g[1], h[0], h[1], g[0])
    y2 = minor(g[2], h[0], h[2], g[0])
    last = minor(s22, s11, s12, s12)
    side = minor(y2, s11, s12, y1)
    alpha = g[0][0] / h[0][0]
    l10 = h[1][0] / h[0][0]
    l20 = h[2][0] / h[0][0]
    l21 = ratio(s12[0], s11[0], l10 + (LOW - SHIFT), l10 + (HIGH - SHIFT))
    gamma1 = ratio(y1[0], s11[0], -alpha / LOW, -alpha / HIGH)
    gamma2 = ratio(side[0], last[0], -gamma1 / HIGH, -gamma1 / LOW)
    c1 = gamma1 - gamma2 * l21
    return alpha - c1 * l10 - gamma2 * l20, c1, gamma2


def sigmoid(value):
    return 1.0 / (1.0 + jnp.exp(-SHARP * value))


def finish_kernel(
    visible_hbm, parts, field, first, second, indicator_hbm, crossing_hbm,
    visible, indicator, crossing, level, weight, sem, slot_sems, result_sem,
):
    nx, ny, nz = indicator.shape
    copy = pltpu.make_async_copy(visible_hbm, visible, sem)
    copy.start()
    devices = parts.shape[0]
    tiles = [parts[pl.ds(8 * k, 8)] for k in range(devices // 8)]
    pairs = [(tile, pltpu.roll(tile, nz - SUMS, 1)) for tile in tiles]
    while len(pairs) > 1:
        pairs = [pair_add(a, b) for a, b in zip(pairs[::2], pairs[1::2])]
    total = pairs[0]
    for step in (4, 2, 1):
        total = pair_add(total, (pltpu.roll(total[0], step, 0), pltpu.roll(total[1], step, 0)))

    def spread(value, k):
        return jnp.broadcast_to(value[0:1, k : k + 1], (1, nz))

    item = [(spread(total[0], k), spread(total[1], k)) for k in range(10)]
    c0, c1, c2 = coefficients(item)
    over = c0 * (item[6][0] + item[6][1]) + c1 * (item[7][0] + item[7][1]) + c2 * (item[8][0] + item[8][1])
    iso = over / item[9][0]

    def set_level(x):
        v0 = field[x + WIDE, pl.ds(EDGE, ny + EDGE)]
        v1 = first[x + NEAR, pl.ds(EDGE + HEM, ny + HEM)]
        v2 = second[x + 1, pl.ds(EDGE + HEM, ny + HEM)]
        value = c0 * v0[: ny + HEM] + c1 * v1 + c2 * v2
        level[x, pl.ds(0, ny + HEM)] = sigmoid(value - iso)
        return value

    @pl.loop(0, nx, unroll=4)
    def _(x):
        indicator[x] = set_level(x)[:ny]

    set_level(nx)
    result = pltpu.make_async_copy(indicator, indicator_hbm, result_sem)
    result.start()
    outside = sigmoid(-iso)
    lane = lax.broadcasted_iota(jnp.int32, (ny, nz), 1)

    @pl.loop(0, nx, unroll=4)
    def _(x):
        here = level[x, pl.ds(0, ny)]
        above = jnp.where(lane < nz - 1, pltpu.roll(here, nz - 1, 1), outside)
        for edge, there in enumerate((level[x + 1, pl.ds(0, ny)], level[x, pl.ds(1, ny)], above)):
            value = here * (1.0 - there) + (1.0 - here) * there
            for row in range(0, ny, 8):
                turned = pltpu.roll(value[row : row + 8], 0, 1, stride=BLK, stride_axis=0)
                weight[edge, pl.ds(x * (ny + 1) + row, 8)] = turned

    chunk = lax.broadcasted_iota(jnp.int32, (8, nz), 1) // BLK
    bricks_z = nz // BLK
    per_row = nz // BLK

    copy.wait()

    def out(slot):
        return pltpu.make_async_copy(crossing.at[slot], crossing_hbm.at[slot], slot_sems.at[slot])

    @pl.loop(0, visible.shape[0], unroll=2)
    def _(slot):
        number = visible[slot]
        safe = jnp.maximum(number, 0)
        begin = (safe // bricks_z) * BLK
        column = safe % bricks_z
        used = jnp.where(number >= 0, 1.0, 0.0)
        spots = [chunk == lax.rem(column + row, per_row) for row in range(per_row)]
        turn = lax.rem(nz - column * BLK, nz)
        for edge in range(3):
            for half in range(2):
                for part in range(BLK // per_row):
                    at = half * 8 * (ny + 1) + begin + part * per_row
                    tile = weight[edge, pl.ds(at, 8, stride=ny + 1)]
                    for row in range(1, per_row):
                        lines = weight[edge, pl.ds(at + row, 8, stride=ny + 1)]
                        tile = jnp.where(spots[row], lines, tile)
                    tile = pltpu.roll(tile, turn, 1) * used
                    crossing[slot, edge, pl.ds(half * 16 + part, 8, stride=2)] = tile
        out(slot).start()

    for slot in range(visible.shape[0]):
        out(slot).wait()
    result.wait()


def whole(*shape):
    return jax.ShapeDtypeStruct(shape, F32)


VMEM = pl.BlockSpec(memory_space=pltpu.VMEM)


HBM = pl.BlockSpec(memory_space=pltpu.HBM)


def kernel(body, inputs, outputs, scratch=(), results=VMEM, alias=None, flops=0):
    return pl.pallas_call(
        body,
        in_specs=list(inputs),
        out_specs=[results] * len(outputs),
        out_shape=list(outputs),
        scratch_shapes=list(scratch),
        input_output_aliases=alias or {},
        cost_estimate=pl.CostEstimate(flops=flops, bytes_accessed=flops // 4, transcendentals=0),
        compiler_params=pltpu.CompilerParams(vmem_limit_bytes=32 * 1024 * 1024),
    )


def in_hbm(value):
    return pltpu.with_memory_space_constraint(value, pltpu.HBM)


def swap(value, axis, first):
    count = lax.axis_size(axis)
    pairs = [(k, k + 1) for k in range(first, count - 1, 2)]
    return lax.ppermute(value, axis, pairs + [(b, a) for a, b in pairs])


def body(right_side, screening, active_blocks, visible_bricks):
    nx, ny, nz = right_side.shape
    active = active_blocks.reshape(-1)
    visible = visible_bricks.reshape(-1)
    devices = lax.axis_size("gx") * lax.axis_size("gy")
    slab = whole(nx, ny, nz)
    planes, near, third = nx + 2 * WIDE, nx + 2 * NEAR, nx + 2
    wide, rows = ny + 2 * EDGE, ny + 2 * HEM
    rim = whole(nx * EDGE, nz)
    edges = pltpu.VMEM((2, nx, EDGE, nz), F32)
    far, near_by, mask = kernel(
        pack_kernel,
        (HBM, HBM, HBM),
        (rim, rim, whole(ny, nz)),
        (pltpu.SMEM(active.shape, jnp.int32), edges, edges, pltpu.SemaphoreType.DMA((5,))),
    )(in_hbm(active), in_hbm(right_side), in_hbm(screening))
    far = swap(far, "gy", 1)
    near_by = swap(near_by, "gy", 0)
    straight, corners = (WIDE + NEAR) * ny, 2 * WIDE * EDGE
    side = whole(straight + corners, nz)
    field, weight, cross, chip = kernel(
        place_kernel,
        (VMEM,) * 3,
        (whole(planes, wide, nz), whole(nx, wide, nz), whole(straight + EXTRA, nz), side),
    )(mask, right_side, screening)
    cross = swap(cross, "gx", 1)
    chip, corner = kernel(widen_kernel, (VMEM,) * 3, (side, whole(corners, nz)), alias={2: 0})(far, near_by, chip)
    chip = swap(chip, "gx", 0)
    corner = swap(corner, "gx", 1)
    kept = [whole(planes, wide, nz)] + [whole(near, wide, nz)] * 2
    kept += [whole(near, rows + 2 * EDGE, nz), whole(third, rows + 2 * EDGE, nz)]
    kept += [whole(planes, rows, nz)] * 2 + [whole(near, rows, nz)] * 2 + [whole(third + 2, ny, nz)] * 2
    tallies = whole(10, 8, nz)
    held = kernel(inner_kernel, (VMEM,) * 4, kept + [tallies], alias={2: 0}, flops=INNER)(
        far, near_by, field, weight
    )
    for last, messages in ((False, (chip, chip)), (True, (cross, corner))):
        held = kernel(
            functools.partial(side_kernel, last),
            (VMEM,) * (HELD + 3),
            kept + [whole(1, nz) if last else tallies],
            alias={2 + k: k for k in range(HELD)},
            flops=SIDE,
        )(*messages, *held)
    field, _, _, first, second = held[:5]
    devices = lax.axis_size("gx") * lax.axis_size("gy")
    parts = lax.all_to_all(jnp.broadcast_to(held[-1], (devices, 1, nz)), ("gx", "gy"), 0, 0)
    slots = visible.shape[0]
    shape = (slots, 3, BLK**3 // nz, nz)
    indicator, crossing = kernel(
        finish_kernel,
        (HBM,) + (VMEM,) * 4,
        (slab, whole(*shape)),
        (
            pltpu.SMEM(visible.shape, jnp.int32),
            pltpu.VMEM(slab.shape, F32),
            pltpu.VMEM(shape, F32),
            pltpu.VMEM((nx + 1, ny + EDGE, nz), F32),
            pltpu.VMEM((3, nx * (ny + 1), nz), F32),
            pltpu.SemaphoreType.DMA,
            pltpu.SemaphoreType.DMA((slots,)),
            pltpu.SemaphoreType.DMA,
        ),
        results=HBM,
    )(in_hbm(visible), parts.reshape(devices, nz), field, first, second)
    return indicator, crossing.reshape(slots, 1, 3, BLK**3)


def solution(mesh):
    return jax.shard_map(
        body,
        mesh=mesh,
        in_specs=(
            P("gx", "gy", None),
            P("gx", "gy", None),
            P("gx", "gy", None),
            P("gx", "gy", None),
        ),
        out_specs=(P("gx", "gy", None), P("gx", "gy", None, None)),
        check_vma=False,
    )
```

profile of v0, /device:TPU:0, one launch (start us, length us, event | category | flops | bytes accessed | tf_op | source)
XLA Modules:
  0.0 31.7 jit_solution(15941699444936410241)
XLA Ops:
  0.6 0.0 copy-start
  0.6 0.0 copy-start.1
  0.6 1.1 %shard_map.59 = (f32[128,128]{1,0:T(8,128)S(1)}, f32[128,128]{1,0:T(8,128)S(1)}, f32[32,128]{1,0:T(8,128)S(1)}) custom-call(s32[12]{0:T(128)} %bitcast.7, f32[16,32,128]{2,1,0:T(8,128)} %right.1, f32[16,32,128]{2,1,0:T(8,128)} %screen.1), custom_call_target="tpu_custom_call" | custom-call | tf_op jit(solution)/shard_map/pallas_call | solution.py:520
  1.7 0.7 %collective-permute-start.1 = (f32[128,128]{1,0:T(8,128)S(1)}, f32[128,128]{1,0:T(8,128)S(1)}, u32[]{:S(2)}, u32[]{:S(2)}) collective-permute-start(f32[128,128]{1,0:T(8,128)S(1)} %get-tuple-element.43), channel_id=1, source_target_pairs={{1,2},{2,1},{5,6},{6,5},{9,10},{10,9},{13,14},{14,13},{17,18},{18,... | collective-permute-start | bytes 196616 | tf_op jit(solution)/shard_map/ppermute | solution.py:507
  2.4 5.7 %collective-permute-start.2 = (f32[128,128]{1,0:T(8,128)S(1)}, f32[128,128]{1,0:T(8,128)S(1)}, u32[]{:S(2)}, u32[]{:S(2)}) collective-permute-start(f32[128,128]{1,0:T(8,128)S(1)} %get-tuple-element.44), channel_id=1, source_target_pairs={{0,1},{2,3},{1,0},{3,2},{4,5},{6,7},{5,4},{7,6},{8,9},{10,11},{9,8... | collective-permute-start | bytes 196616 | tf_op jit(solution)/shard_map/ppermute | solution.py:507
  8.1 0.0 copy-done
  8.1 0.0 copy-done.1
  8.1 0.1 shard_map.60
  8.2 0.7 %collective-permute-start = (f32[352,128]{1,0:T(8,128)S(1)}, f32[352,128]{1,0:T(8,128)S(1)}, u32[]{:S(2)}, u32[]{:S(2)}) collective-permute-start(f32[352,128]{1,0:T(8,128)S(1)} %get-tuple-element.42), channel_id=1, source_target_pairs={{4,8},{12,16},{20,24},{8,4},{16,12},{24,20},{5,9},{13,17},{21,25},... | collective-permute-start | bytes 540680 | tf_op jit(solution)/shard_map/ppermute | solution.py:507
  8.9 0.0 collective-permute-done.1.far
  8.9 2.4 %collective-permute-done.2.near = f32[128,128]{1,0:T(8,128)S(1)} collective-permute-done((f32[128,128]{1,0:T(8,128)S(1)}, f32[128,128]{1,0:T(8,128)S(1)}, u32[]{:S(2)}, u32[]{:S(2)}) %collective-permute-start.2) | collective-permute-done | bytes 65568 | tf_op jit(solution)/shard_map/ppermute | solution.py:507
  11.3 0.7 %collective-permute-start.4 = (f32[336,128]{1,0:T(8,128)S(1)}, f32[336,128]{1,0:T(8,128)S(1)}, u32[]{:S(2)}, u32[]{:S(2)}) collective-permute-start(f32[336,128]{1,0:T(8,128)S(1)} %get-tuple-element.47), channel_id=1, source_target_pairs={{0,4},{8,12},{16,20},{24,28},{4,0},{12,8},{20,16},{28,24},{1,5},{9... | collective-permute-start | bytes 516104 | tf_op jit(solution)/shard_map/ppermute | solution.py:507
  11.9 0.7 %collective-permute-start.3 = (f32[80,128]{1,0:T(8,128)S(1)}, f32[80,128]{1,0:T(8,128)S(1)}, u32[]{:S(2)}, u32[]{:S(2)}) collective-permute-start(f32[80,128]{1,0:T(8,128)S(1)} %get-tuple-element.46), channel_id=1, source_target_pairs={{4,8},{12,16},{20,24},{8,4},{16,12},{24,20},{5,9},{13,17},{21,25},... | collective-permute-start | bytes 122888 | tf_op jit(solution)/shard_map/ppermute | solution.py:507
  12.6 1.6 %shard_map.62 = (f32[26,48,128]{2,1,0:T(8,128)S(1)}, f32[22,48,128]{2,1,0:T(8,128)S(1)}, f32[22,48,128]{2,1,0:T(8,128)S(1)}, f32[22,56,128]{2,1,0:T(8,128)S(1)},...) custom-call(f32[128,128]{1,0:T(8,128)S(1)} %collective-permute-done., ...), custom_call_target="tpu_custom_call", output_to_operand_aliasing={{0}: (2, {})} | custom-call | tf_op jit(solution)/shard_map/pallas_call | solution.py:543
  14.2 0.0 collective-permute-done.4.message.corner
  14.2 0.8 %shard_map.63 = (f32[26,48,128]{2,1,0:T(8,128)S(1)}, f32[22,48,128]{2,1,0:T(8,128)S(1)}, f32[22,48,128]{2,1,0:T(8,128)S(1)}, f32[22,56,128]{2,1,0:T(8,128)S(1)},...) custom-call(f32[336,128]{1,0:T(8,128)S(1)} %collective-permute-done., ...), custom_call_target="tpu_custom_call", output_to_operand_aliasing={{0}: (2, {}), {1}: (3, {}), {2}: (4, {}), {3}: (5, {}), {4}... | custom-call | tf_op jit(solution)/shard_map/pallas_call | solution.py:547
  15.0 0.0 collective-permute-done.3.corner
  15.0 0.0 collective-permute-done.message
  15.0 1.0 %shard_map.64 = (f32[26,48,128]{2,1,0:T(8,128)S(1)}, f32[22,48,128]{2,1,0:T(8,128)S(1)}, f32[22,48,128]{2,1,0:T(8,128)S(1)}, f32[22,56,128]{2,1,0:T(8,128)S(1)},...) custom-call(f32[352,128]{1,0:T(8,128)S(1)} %collective-permute-done., ...), custom_call_target="tpu_custom_call", output_to_operand_aliasing={{0}: (2, {}), {1}: (3, {}), {2}: (4, {}), {3}: (5, {}), {4}... | custom-call | tf_op jit(solution)/shard_map/pallas_call | solution.py:547
  16.0 13.4 %all_to_all.5 = f32[32,1,128]{2,1,0:T(1,128)S(1)} all-to-all(f32[32,1,128]{2,1,0:T(1,128)S(1)} %broadcast_in_dim.3), channel_id=1, replica_groups=mesh['gx'=8,'gy'=4] {'gx','gy'}, dimensions={0} | all-to-all | bytes 32768 | tf_op jit(solution)/shard_map/all_to_all | solution.py:556
  29.4 2.3 %shard_map.65 = (f32[16,32,128]{2,1,0:T(8,128)}, f32[8,3,32,128]{3,2,1,0:T(8,128)}) custom-call(s32[8]{0:T(128)} %bitcast.8, f32[32,128]{1,0:T(8,128)S(1)} %bitcast.5, f32[26,48,128]{2,1,0:T(8,128)S(1)} %get-tuple-element.75.field, f32[22,56,128]{2,1,0:T(8,128)S(1)} %get-tuple-element.76.first, f32[18,56,128]{2,1,0:T(8,128)S(1)} %get-tuple-element.77.second), custom_call_target="tpu_custom_call" | custom-call | tf_op jit(solution)/shard_map/pallas_call | solution.py:559
  (2 shorter events, 0.0 us)
Async XLA Ops:
  0.6 7.5 %copy-start = (f32[16,32,128]{2,1,0:T(8,128)S(1)}, f32[16,32,128]{2,1,0:T(8,128)}, u32[]{:S(2)}) copy-start(f32[16,32,128]{2,1,0:T(8,128)} %right.1) | copy-start | bytes 786436
  0.6 7.5 %copy-start.1 = (f32[16,32,128]{2,1,0:T(8,128)S(1)}, f32[16,32,128]{2,1,0:T(8,128)}, u32[]{:S(2)}) copy-start(f32[16,32,128]{2,1,0:T(8,128)} %screen.1) | copy-start | bytes 786436
  1.7 7.2 %collective-permute-start.1 = (f32[128,128]{1,0:T(8,128)S(1)}, f32[128,128]{1,0:T(8,128)S(1)}, u32[]{:S(2)}, u32[]{:S(2)}) collective-permute-start(f32[128,128]{1,0:T(8,128)S(1)} %get-tuple-element.43), channel_id=1, source_target_pairs={{1,2},{2,1},{5,6},{6,5},{9,10},{10,9},{13,14},{14,13},{17,18},{18,... | collective-permute-start | bytes 196616 | tf_op jit(solution)/shard_map/ppermute | solution.py:507
  2.4 8.9 %collective-permute-start.2 = (f32[128,128]{1,0:T(8,128)S(1)}, f32[128,128]{1,0:T(8,128)S(1)}, u32[]{:S(2)}, u32[]{:S(2)}) collective-permute-start(f32[128,128]{1,0:T(8,128)S(1)} %get-tuple-element.44), channel_id=1, source_target_pairs={{0,1},{2,3},{1,0},{3,2},{4,5},{6,7},{5,4},{7,6},{8,9},{10,11},{9,8... | collective-permute-start | bytes 196616 | tf_op jit(solution)/shard_map/ppermute | solution.py:507
  8.2 6.8 %collective-permute-start = (f32[352,128]{1,0:T(8,128)S(1)}, f32[352,128]{1,0:T(8,128)S(1)}, u32[]{:S(2)}, u32[]{:S(2)}) collective-permute-start(f32[352,128]{1,0:T(8,128)S(1)} %get-tuple-element.42), channel_id=1, source_target_pairs={{4,8},{12,16},{20,24},{8,4},{16,12},{24,20},{5,9},{13,17},{21,25},... | collective-permute-start | bytes 540680 | tf_op jit(solution)/shard_map/ppermute | solution.py:507
  11.3 2.9 %collective-permute-start.4 = (f32[336,128]{1,0:T(8,128)S(1)}, f32[336,128]{1,0:T(8,128)S(1)}, u32[]{:S(2)}, u32[]{:S(2)}) collective-permute-start(f32[336,128]{1,0:T(8,128)S(1)} %get-tuple-element.47), channel_id=1, source_target_pairs={{0,4},{8,12},{16,20},{24,28},{4,0},{12,8},{20,16},{28,24},{1,5},{9... | collective-permute-start | bytes 516104 | tf_op jit(solution)/shard_map/ppermute | solution.py:507
  11.9 3.1 %collective-permute-start.3 = (f32[80,128]{1,0:T(8,128)S(1)}, f32[80,128]{1,0:T(8,128)S(1)}, u32[]{:S(2)}, u32[]{:S(2)}) collective-permute-start(f32[80,128]{1,0:T(8,128)S(1)} %get-tuple-element.46), channel_id=1, source_target_pairs={{4,8},{12,16},{20,24},{8,4},{16,12},{24,20},{5,9},{13,17},{21,25},... | collective-permute-start | bytes 122888 | tf_op jit(solution)/shard_map/ppermute | solution.py:507
where the time goes:
time: 31.9 us; the launch traced here: 31.7 us
  blocking collectives  13.4 us (42%)
  starting transfers between devices  8.39 us (26%)
  Pallas kernels  6.78 us (21%)
  waiting for transfers between devices  2.38 us (7%)
  between operations  0.74 us (2%)
    all_to_all x1, blocking collectives, body(): lax.all_to_all(jnp.broadcast_to(held[-1], (devices, 1, nz)), ('gx', 'gy')...  13.4 us
    ppermute x5, starting transfers between devices, swap(): return lax.ppermute(value, axis, pairs + [(b, a) for a, b in pairs])  8.39 us
    ppermute x5, waiting for transfers between devices, swap(): return lax.ppermute(value, axis, pairs + [(b, a) for a, b in pairs])  2.38 us
    pallas_call x1, Pallas kernels, body(): kernel(finish_kernel, (HBM,) + (VMEM,) * 4, (slab, whole(*shape)), (pltpu...  2.32 us
    pallas_call x2, Pallas kernels, body(): kernel(functools.partial(side_kernel, last), (VMEM,) * (HELD + 3), kept +...  1.74 us
    pallas_call x1, Pallas kernels, body(): kernel(inner_kernel, (VMEM,) * 4, kept + [tallies], alias={2: 0}, flops=I...  1.6 us
    pallas_call x1, Pallas kernels, body(): kernel(pack_kernel, (HBM, HBM, HBM), (rim, rim, whole(ny, nz)), (pltpu.SM...  1.06 us
  transfers between devices with their start and end apart: 5, of which 1 were waited for; matrix products, arithmetic and copies ran while one was open for 0% of the time, Pallas kernels for 8%

commit v1 on v0

--- a/solution.py
+++ b/solution.py
@@ -419,8 +419,7 @@
         level[x, pl.ds(0, ny + HEM)] = sigmoid(value - iso)
         return value
 
-    @pl.loop(0, nx, unroll=4)
-    def _(x):
+    for x in range(nx):
         indicator[x] = set_level(x)[:ny]
 
     set_level(nx)
@@ -429,8 +428,7 @@
     outside = sigmoid(-iso)
     lane = lax.broadcasted_iota(jnp.int32, (ny, nz), 1)
 
-    @pl.loop(0, nx, unroll=4)
-    def _(x):
+    for x in range(nx):
         here = level[x, pl.ds(0, ny)]
         above = jnp.where(lane < nz - 1, pltpu.roll(here, nz - 1, 1), outside)
         for edge, there in enumerate((level[x + 1, pl.ds(0, ny)], level[x, pl.ds(1, ny)], above)):
@@ -448,13 +446,11 @@
     def out(slot):
         return pltpu.make_async_copy(crossing.at[slot], crossing_hbm.at[slot], slot_sems.at[slot])
 
-    @pl.loop(0, visible.shape[0], unroll=2)
-    def _(slot):
+    for slot in range(visible.shape[0]):
         number = visible[slot]
         safe = jnp.maximum(number, 0)
         begin = (safe // bricks_z) * BLK
         column = safe % bricks_z
-        used = jnp.where(number >= 0, 1.0, 0.0)
         spots = [chunk == lax.rem(column + row, per_row) for row in range(per_row)]
         turn = lax.rem(nz - column * BLK, nz)
         for edge in range(3):
@@ -465,7 +461,7 @@
                     for row in range(1, per_row):
                         lines = weight[edge, pl.ds(at + row, 8, stride=ny + 1)]
                         tile = jnp.where(spots[row], lines, tile)
-                    tile = pltpu.roll(tile, turn, 1) * used
+                    tile = jnp.where(number >= 0, pltpu.roll(tile, turn, 1), 0.0)
                     crossing[slot, edge, pl.ds(half * 16 + part, 8, stride=2)] = tile
         out(slot).start()
 

time: 31.9 us -> 31.8 us (level)
  no operation moved by 1% of the time
where the time goes in v1:
time: 31.8 us; the launch traced here: 31.6 us
  blocking collectives  13.4 us (42%)
  starting transfers between devices  8.39 us (26%)
  Pallas kernels  6.64 us (21%)
  waiting for transfers between devices  2.38 us (7%)
  between operations  0.74 us (2%)
    all_to_all x1, blocking collectives, body(): lax.all_to_all(jnp.broadcast_to(held[-1], (devices, 1, nz)), ('gx', 'gy')...  13.4 us
    ppermute x5, starting transfers between devices, swap(): return lax.ppermute(value, axis, pairs + [(b, a) for a, b in pairs])  8.39 us
    ppermute x5, waiting for transfers between devices, swap(): return lax.ppermute(value, axis, pairs + [(b, a) for a, b in pairs])  2.38 us
    pallas_call x1, Pallas kernels, body(): kernel(finish_kernel, (HBM,) + (VMEM,) * 4, (slab, whole(*shape)), (pltpu...  2.18 us
    pallas_call x2, Pallas kernels, body(): kernel(functools.partial(side_kernel, last), (VMEM,) * (HELD + 3), kept +...  1.74 us
    pallas_call x1, Pallas kernels, body(): kernel(inner_kernel, (VMEM,) * 4, kept + [tallies], alias={2: 0}, flops=I...  1.6 us
    pallas_call x1, Pallas kernels, body(): kernel(pack_kernel, (HBM, HBM, HBM), (rim, rim, whole(ny, nz)), (pltpu.SM...  1.06 us
  transfers between devices with their start and end apart: 5, of which 1 were waited for; matrix products, arithmetic and copies ran while one was open for 0% of the time, Pallas kernels for 8%

profile of v1, /device:TPU:0, one launch (start us, length us, event | category | flops | bytes accessed | tf_op | source)
XLA Modules:
  0.0 31.6 jit_solution(3290395972181812190)
XLA Ops:
  0.6 0.0 copy-start
  0.6 0.0 copy-start.1
  0.6 1.1 %shard_map.59 = (f32[128,128]{1,0:T(8,128)S(1)}, f32[128,128]{1,0:T(8,128)S(1)}, f32[32,128]{1,0:T(8,128)S(1)}) custom-call(s32[12]{0:T(128)} %bitcast.7, f32[16,32,128]{2,1,0:T(8,128)} %right.1, f32[16,32,128]{2,1,0:T(8,128)} %screen.1), custom_call_target="tpu_custom_call" | custom-call | tf_op jit(solution)/shard_map/pallas_call | solution.py:516
  1.7 0.7 %collective-permute-start.1 = (f32[128,128]{1,0:T(8,128)S(1)}, f32[128,128]{1,0:T(8,128)S(1)}, u32[]{:S(2)}, u32[]{:S(2)}) collective-permute-start(f32[128,128]{1,0:T(8,128)S(1)} %get-tuple-element.43), channel_id=1, source_target_pairs={{1,2},{2,1},{5,6},{6,5},{9,10},{10,9},{13,14},{14,13},{17,18},{18,... | collective-permute-start | bytes 196616 | tf_op jit(solution)/shard_map/ppermute | solution.py:503
  2.4 5.7 %collective-permute-start.2 = (f32[128,128]{1,0:T(8,128)S(1)}, f32[128,128]{1,0:T(8,128)S(1)}, u32[]{:S(2)}, u32[]{:S(2)}) collective-permute-start(f32[128,128]{1,0:T(8,128)S(1)} %get-tuple-element.44), channel_id=1, source_target_pairs={{0,1},{2,3},{1,0},{3,2},{4,5},{6,7},{5,4},{7,6},{8,9},{10,11},{9,8... | collective-permute-start | bytes 196616 | tf_op jit(solution)/shard_map/ppermute | solution.py:503
  8.1 0.0 copy-done
  8.1 0.0 copy-done.1
  8.1 0.1 shard_map.60
  8.2 0.7 %collective-permute-start = (f32[352,128]{1,0:T(8,128)S(1)}, f32[352,128]{1,0:T(8,128)S(1)}, u32[]{:S(2)}, u32[]{:S(2)}) collective-permute-start(f32[352,128]{1,0:T(8,128)S(1)} %get-tuple-element.42), channel_id=1, source_target_pairs={{4,8},{12,16},{20,24},{8,4},{16,12},{24,20},{5,9},{13,17},{21,25},... | collective-permute-start | bytes 540680 | tf_op jit(solution)/shard_map/ppermute | solution.py:503
  8.9 0.0 collective-permute-done.1.far
  8.9 2.4 %collective-permute-done.2.near = f32[128,128]{1,0:T(8,128)S(1)} collective-permute-done((f32[128,128]{1,0:T(8,128)S(1)}, f32[128,128]{1,0:T(8,128)S(1)}, u32[]{:S(2)}, u32[]{:S(2)}) %collective-permute-start.2) | collective-permute-done | bytes 65568 | tf_op jit(solution)/shard_map/ppermute | solution.py:503
  11.3 0.7 %collective-permute-start.4 = (f32[336,128]{1,0:T(8,128)S(1)}, f32[336,128]{1,0:T(8,128)S(1)}, u32[]{:S(2)}, u32[]{:S(2)}) collective-permute-start(f32[336,128]{1,0:T(8,128)S(1)} %get-tuple-element.47), channel_id=1, source_target_pairs={{0,4},{8,12},{16,20},{24,28},{4,0},{12,8},{20,16},{28,24},{1,5},{9... | collective-permute-start | bytes 516104 | tf_op jit(solution)/shard_map/ppermute | solution.py:503
  11.9 0.7 %collective-permute-start.3 = (f32[80,128]{1,0:T(8,128)S(1)}, f32[80,128]{1,0:T(8,128)S(1)}, u32[]{:S(2)}, u32[]{:S(2)}) collective-permute-start(f32[80,128]{1,0:T(8,128)S(1)} %get-tuple-element.46), channel_id=1, source_target_pairs={{4,8},{12,16},{20,24},{8,4},{16,12},{24,20},{5,9},{13,17},{21,25},... | collective-permute-start | bytes 122888 | tf_op jit(solution)/shard_map/ppermute | solution.py:503
  12.6 1.6 %shard_map.62 = (f32[26,48,128]{2,1,0:T(8,128)S(1)}, f32[22,48,128]{2,1,0:T(8,128)S(1)}, f32[22,48,128]{2,1,0:T(8,128)S(1)}, f32[22,56,128]{2,1,0:T(8,128)S(1)},...) custom-call(f32[128,128]{1,0:T(8,128)S(1)} %collective-permute-done., ...), custom_call_target="tpu_custom_call", output_to_operand_aliasing={{0}: (2, {})} | custom-call | tf_op jit(solution)/shard_map/pallas_call | solution.py:539
  14.2 0.0 collective-permute-done.4.message.corner
  14.2 0.8 %shard_map.63 = (f32[26,48,128]{2,1,0:T(8,128)S(1)}, f32[22,48,128]{2,1,0:T(8,128)S(1)}, f32[22,48,128]{2,1,0:T(8,128)S(1)}, f32[22,56,128]{2,1,0:T(8,128)S(1)},...) custom-call(f32[336,128]{1,0:T(8,128)S(1)} %collective-permute-done., ...), custom_call_target="tpu_custom_call", output_to_operand_aliasing={{0}: (2, {}), {1}: (3, {}), {2}: (4, {}), {3}: (5, {}), {4}... | custom-call | tf_op jit(solution)/shard_map/pallas_call | solution.py:543
  15.0 0.0 collective-permute-done.3.corner
  15.0 0.0 collective-permute-done.message
  15.0 1.0 %shard_map.64 = (f32[26,48,128]{2,1,0:T(8,128)S(1)}, f32[22,48,128]{2,1,0:T(8,128)S(1)}, f32[22,48,128]{2,1,0:T(8,128)S(1)}, f32[22,56,128]{2,1,0:T(8,128)S(1)},...) custom-call(f32[352,128]{1,0:T(8,128)S(1)} %collective-permute-done., ...), custom_call_target="tpu_custom_call", output_to_operand_aliasing={{0}: (2, {}), {1}: (3, {}), {2}: (4, {}), {3}: (5, {}), {4}... | custom-call | tf_op jit(solution)/shard_map/pallas_call | solution.py:543
  16.0 13.4 %all_to_all.5 = f32[32,1,128]{2,1,0:T(1,128)S(1)} all-to-all(f32[32,1,128]{2,1,0:T(1,128)S(1)} %broadcast_in_dim.3), channel_id=1, replica_groups=mesh['gx'=8,'gy'=4] {'gx','gy'}, dimensions={0} | all-to-all | bytes 32768 | tf_op jit(solution)/shard_map/all_to_all | solution.py:552
  29.4 2.2 %shard_map.65 = (f32[16,32,128]{2,1,0:T(8,128)}, f32[8,3,32,128]{3,2,1,0:T(8,128)}) custom-call(s32[8]{0:T(128)} %bitcast.8, f32[32,128]{1,0:T(8,128)S(1)} %bitcast.5, f32[26,48,128]{2,1,0:T(8,128)S(1)} %get-tuple-element.75.field, f32[22,56,128]{2,1,0:T(8,128)S(1)} %get-tuple-element.76.first, f32[18,56,128]{2,1,0:T(8,128)S(1)} %get-tuple-element.77.second), custom_call_target="tpu_custom_call" | custom-call | tf_op jit(solution)/shard_map/pallas_call | solution.py:555
  (2 shorter events, 0.0 us)
Async XLA Ops:
  0.6 7.5 %copy-start = (f32[16,32,128]{2,1,0:T(8,128)S(1)}, f32[16,32,128]{2,1,0:T(8,128)}, u32[]{:S(2)}) copy-start(f32[16,32,128]{2,1,0:T(8,128)} %right.1) | copy-start | bytes 786436
  0.6 7.5 %copy-start.1 = (f32[16,32,128]{2,1,0:T(8,128)S(1)}, f32[16,32,128]{2,1,0:T(8,128)}, u32[]{:S(2)}) copy-start(f32[16,32,128]{2,1,0:T(8,128)} %screen.1) | copy-start | bytes 786436
  1.7 7.2 %collective-permute-start.1 = (f32[128,128]{1,0:T(8,128)S(1)}, f32[128,128]{1,0:T(8,128)S(1)}, u32[]{:S(2)}, u32[]{:S(2)}) collective-permute-start(f32[128,128]{1,0:T(8,128)S(1)} %get-tuple-element.43), channel_id=1, source_target_pairs={{1,2},{2,1},{5,6},{6,5},{9,10},{10,9},{13,14},{14,13},{17,18},{18,... | collective-permute-start | bytes 196616 | tf_op jit(solution)/shard_map/ppermute | solution.py:503
  2.4 8.9 %collective-permute-start.2 = (f32[128,128]{1,0:T(8,128)S(1)}, f32[128,128]{1,0:T(8,128)S(1)}, u32[]{:S(2)}, u32[]{:S(2)}) collective-permute-start(f32[128,128]{1,0:T(8,128)S(1)} %get-tuple-element.44), channel_id=1, source_target_pairs={{0,1},{2,3},{1,0},{3,2},{4,5},{6,7},{5,4},{7,6},{8,9},{10,11},{9,8... | collective-permute-start | bytes 196616 | tf_op jit(solution)/shard_map/ppermute | solution.py:503
  8.2 6.8 %collective-permute-start = (f32[352,128]{1,0:T(8,128)S(1)}, f32[352,128]{1,0:T(8,128)S(1)}, u32[]{:S(2)}, u32[]{:S(2)}) collective-permute-start(f32[352,128]{1,0:T(8,128)S(1)} %get-tuple-element.42), channel_id=1, source_target_pairs={{4,8},{12,16},{20,24},{8,4},{16,12},{24,20},{5,9},{13,17},{21,25},... | collective-permute-start | bytes 540680 | tf_op jit(solution)/shard_map/ppermute | solution.py:503
  11.3 2.9 %collective-permute-start.4 = (f32[336,128]{1,0:T(8,128)S(1)}, f32[336,128]{1,0:T(8,128)S(1)}, u32[]{:S(2)}, u32[]{:S(2)}) collective-permute-start(f32[336,128]{1,0:T(8,128)S(1)} %get-tuple-element.47), channel_id=1, source_target_pairs={{0,4},{8,12},{16,20},{24,28},{4,0},{12,8},{20,16},{28,24},{1,5},{9... | collective-permute-start | bytes 516104 | tf_op jit(solution)/shard_map/ppermute | solution.py:503
  11.9 3.1 %collective-permute-start.3 = (f32[80,128]{1,0:T(8,128)S(1)}, f32[80,128]{1,0:T(8,128)S(1)}, u32[]{:S(2)}, u32[]{:S(2)}) collective-permute-start(f32[80,128]{1,0:T(8,128)S(1)} %get-tuple-element.46), channel_id=1, source_target_pairs={{4,8},{12,16},{20,24},{8,4},{16,12},{24,20},{5,9},{13,17},{21,25},... | collective-permute-start | bytes 122888 | tf_op jit(solution)/shard_map/ppermute | solution.py:503
